TPU v7x, 32 devices: a whole 2x2x4 slice. The times are simulated.
32 devices in a mesh: ctx: 16 (over z, y, core), tp: 2 (over x).
Axes of the slice: x: 2, y: 2, z: 4, core: 2. Of those that a mesh axis runs over, the one named last changes fastest.
Arguments:
- queries: bfloat16 [4096, 4096], P('ctx', 'tp'), may hold values from -112 to 112
- keys: bfloat16 [4096, 1024], P('ctx', 'tp'), may hold values from -4.5 to 4.5
- values: bfloat16 [4096, 1024], P('ctx', 'tp'), may hold values from -6 to 6
- head_kind: int32 [8], replicated, may hold values from 0 to 1, as said below
- sink_len: int32 [8], replicated, may hold values from 32 to 128, as said below
- window_len: int32 [8], replicated, may hold values from 512 to 1024, as said below
- w_out: bfloat16 [4096, 4096], P('tp'), may hold values from -0.375 to 0.375
Outputs:
- mixed: bfloat16 [4096, 4096], P(('ctx', 'tp'))
Inputs may be any that keep to these rules, and one draw needn't show every extreme that they name: `head_kind`: exactly 4 entries are 1. `sink_len`: some head with head_kind 0 has exactly 128. `window_len`: some head with head_kind 0 has exactly 1024.
All inputs are finite; a program needn't handle non-finite values.
Results may differ from a plain program's by a relative error of at most 0.014.
Values may be sent and summed in bfloat16 or wider, within the bound.
A program may use at most 128 MiB of HBM per device.

v0:
```python
import math

import jax
import jax.numpy as jnp
from jax import lax
from jax.sharding import PartitionSpec as P

HD = 128
SINK = 128


start_max = -1e30


def spread(block, axis, holder):
    block = jnp.where(lax.axis_index(axis) == holder, block, jnp.zeros_like(block))
    return lax.psum(block, axis)


def from_behind(shard, axis, by):
    count = lax.axis_size(axis)
    pairs = [(i, i + by) for i in range(count) if 0 <= i + by < count]
    return lax.ppermute(shard, axis, pairs)


def softmax_update(carry_state, query_rows, key_rows, value_rows, mask_rows, score_scale):
    running_max, running_sum, running_acc = carry_state
    scores = (
        jnp.einsum("rgd,kd->rgk", query_rows, key_rows, preferred_element_type=jnp.float32)
        * score_scale
    )
    masked = jnp.where(mask_rows, scores, -jnp.inf)
    new_max = jnp.maximum(running_max, jnp.max(masked, axis=2))
    weights = jnp.where(mask_rows, jnp.exp(scores - new_max[:, :, None]), 0.0)
    factor = jnp.exp(running_max - new_max)
    new_sum = running_sum * factor + jnp.sum(weights, axis=2)
    new_acc = running_acc * factor[:, :, None] + jnp.einsum(
        "rgk,kd->rgd", weights.astype(jnp.bfloat16), value_rows, preferred_element_type=jnp.float32
    )
    return (new_max, new_sum, new_acc)


def empty_state(row_count, group_size):
    return (
        jnp.full((row_count, group_size), start_max, jnp.float32),
        jnp.zeros((row_count, group_size), jnp.float32),
        jnp.zeros((row_count, group_size, HD), jnp.float32),
    )


def body(queries, keys, values, head_kind, sink_len, window_len, w_out):
    rows_here = queries.shape[0]
    local_kv = keys.shape[1] // HD
    group_size = queries.shape[1] // keys.shape[1]
    ctx_rank = lax.axis_index("ctx")
    tp_rank = lax.axis_index("tp")
    score_scale = 1.0 / math.sqrt(HD)
    first_head = tp_rank * local_kv
    local_kinds = lax.dynamic_slice_in_dim(head_kind, first_head, local_kv)
    local_sinks = lax.dynamic_slice_in_dim(sink_len, first_head, local_kv)
    local_windows = lax.dynamic_slice_in_dim(window_len, first_head, local_kv)
    kv_pairs = jnp.concatenate([keys, values], axis=1)
    row_ids = jnp.arange(rows_here, dtype=jnp.int32)
    own_pos = ctx_rank * rows_here + row_ids
    heads_q = queries.reshape(rows_here, local_kv, group_size, HD)
    sink_rows = spread(kv_pairs[:SINK], "ctx", 0)
    earlier = [from_behind(kv_pairs, "ctx", distance) for distance in (4, 3, 2, 1)]
    recent = jnp.concatenate(earlier + [kv_pairs], axis=0)
    window_keys = jnp.concatenate([sink_rows, recent], axis=0)
    recent_pos = (ctx_rank - 4) * rows_here + jnp.arange(5 * rows_here, dtype=jnp.int32)
    sink_pos = jnp.arange(SINK, dtype=jnp.int32)
    query_pos = own_pos[:, None]
    window_out = []
    for kv_head in range(local_kv):
        in_window = (
            (recent_pos[None, :] <= query_pos)
            & (recent_pos[None, :] > query_pos - local_windows[kv_head])
            & (recent_pos[None, :] >= local_sinks[kv_head])
        )
        in_sink = (sink_pos[None, :] < local_sinks[kv_head]) & (sink_pos[None, :] <= query_pos)
        allowed = jnp.concatenate([in_sink, in_window], axis=1)[:, None, :]
        key_cols = window_keys[:, kv_head * HD : (kv_head + 1) * HD]
        value_cols = window_keys[:, (local_kv + kv_head) * HD : (local_kv + kv_head + 1) * HD]
        result = lax.cond(
            local_kinds[kv_head] == 0,
            lambda operand, query_rows=heads_q[
                :, kv_head
            ], key_rows=key_cols, value_rows=value_cols, mask_rows=allowed: softmax_update(
                operand, query_rows, key_rows, value_rows, mask_rows, score_scale
            ),
            lambda operand: operand,
            empty_state(rows_here, group_size),
        )
        window_out.append(
            jnp.where(local_kinds[kv_head] == 0, result[2] / result[1][:, :, None], 0.0)
        )
    window_all = jnp.stack(window_out, axis=1).astype(jnp.bfloat16)
    ret_heads = queries.reshape(rows_here, local_kv, group_size, HD)
    half_rows = rows_here // 2
    block_top = [jnp.max(own_pos[:half_rows]), jnp.max(own_pos[half_rows:])]
    tasks = [
        (ret_heads[:, slot], slot, local_kv + slot, local_kinds[slot] == 1)
        for slot in range(local_kv)
    ]
    initial = tuple((empty_state(rows_here, task[0].shape[1]) for task in tasks))
    piece_rows = lax.all_gather(kv_pairs, "ctx", axis=0, tiled=True)
    piece_count = piece_rows.shape[0]
    block_span = math.gcd(piece_count, 4 * rows_here)

    def key_step(block_index, state_all):
        block_begin = block_index * block_span
        key_block = lax.dynamic_slice_in_dim(piece_rows, block_begin, block_span, 0)
        key_pos = block_begin + jnp.arange(block_span, dtype=jnp.int32)
        updated = []
        for task_index in range(len(tasks)):
            task_q, key_index, value_index, task_flag = tasks[task_index]
            key_cols = key_block[:, key_index * HD : (key_index + 1) * HD]
            value_cols = key_block[:, value_index * HD : (value_index + 1) * HD]
            current = state_all[task_index]
            for which_half in range(2):
                lower_row = which_half * half_rows
                upper_row = lower_row + half_rows
                allowed = (key_pos[None, :] <= own_pos[lower_row:upper_row, None])[:, None, :]
                needed = task_flag & (block_begin <= block_top[which_half])
                sliced = tuple((member[lower_row:upper_row] for member in current))
                result = lax.cond(
                    needed,
                    lambda operand, query_rows=task_q[
                        lower_row:upper_row
                    ], key_rows=key_cols, value_rows=value_cols, mask_rows=allowed: softmax_update(
                        operand, query_rows, key_rows, value_rows, mask_rows, score_scale
                    ),
                    lambda operand: operand,
                    sliced,
                )
                current = tuple(
                    (
                        member.at[lower_row:upper_row].set(piece)
                        for member, piece in zip(current, result)
                    )
                )
            updated.append(current)
        return tuple(updated)

    folded = lax.fori_loop(0, piece_count // block_span, key_step, initial)
    finished = [
        jnp.where(
            tasks[task_index][3], folded[task_index][2] / folded[task_index][1][:, :, None], 0.0
        ).astype(jnp.bfloat16)
        for task_index in range(len(tasks))
    ]
    ret_out = jnp.stack(finished, axis=1)
    attention = jnp.where((local_kinds == 1)[None, :, None, None], ret_out, window_all).reshape(
        rows_here, local_kv * group_size * HD
    )
    return lax.psum_scatter(
        jnp.dot(attention, w_out, preferred_element_type=jnp.float32).astype(jnp.bfloat16),
        "tp",
        scatter_dimension=0,
        tiled=True,
    )


def solution(mesh):
    in_specs = (P("ctx", "tp"), P("ctx", "tp"), P("ctx", "tp"), P(), P(), P(), P("tp", None))
    out_specs = P(("ctx", "tp"), None)
    return jax.shard_map(body, mesh=mesh, in_specs=in_specs, out_specs=out_specs, check_vma=False)
```

profile of v0, /device:TPU:24, one launch (start us, length us, event | category | flops | bytes accessed | tf_op | source)
XLA Modules:
  0.0 323.8 jit_solution(11626235243320493928)
XLA Ops:
  11.5 2.9 collective-permute-start.1
  14.4 1.9 collective-permute-start.2
  16.3 1.9 collective-permute-start.3
  39.6 65.5 %all-reduce.2.cloned.1.call-done = bf16[128,1024]{1,0:T(8,128)(2,1)} async-done(((bf16[128,1024]{1,0:T(8,128)(2,1)}), bf16[128,1024]{1,0:T(8,128)(2,1)}) %all-reduce.2.cloned.1.call-update) | async-done | bytes 262160 | tf_op jit(solution)/shard_map/psum | solution.py:17
  105.1 1.7 constant_dynamic-update-slice_fusion.31
  106.8 1.9 constant_dynamic-update-slice_fusion.30
  108.8 1.9 constant_dynamic-update-slice_fusion.29
  110.7 1.9 constant_dynamic-update-slice_fusion.28
  112.6 1.9 constant_dynamic-update-slice_fusion.27
  116.0 9.5 %conditional.14 = (f32[256,4]{0,1:T(4,128)S(1)}, f32[256,4,128]{0,2,1:T(8,128)}) conditional(s32[]{:T(128)} %convert_element_type.162, () %tuple.315, (pred[256,1408]{1,0:T(8,128)(4,1)S(1)}, bf16[1408,1024]{1,0:T(8,128)(2,1)}, bf16[256,4,128]{0,2,1:T(8,128)(2,1)S(1)}) %tuple.316), branch_computations={%region_45.46_spmd, %region_46.49_spmd} | conditional | flops 754191360 | bytes 20983824 | solution.py:84
  116.0 2.5 select_reduce_fusion.10
  118.5 1.7 fusion.129
  120.2 3.2 fusion.133
  123.4 2.0 copy.38
  128.1 52.4 %all-gather.2.cloned.1.call-done = bf16[4096,1024]{1,0:T(8,128)(2,1)} async-done(((bf16[256,1024]{1,0:T(8,128)(2,1)}), bf16[4096,1024]{1,0:T(8,128)(2,1)}) %all-gather.2.cloned.1.call-update) | async-done | bytes 8388624 | tf_op jit(solution)/shard_map/all_gather | solution.py:106
  181.6 88.8 %while.62 = (s32[]{:T(128)}, f32[256,4]{0,1:T(4,128)S(1)}, f32[256,4]{0,1:T(4,128)S(1)}, f32[256,4,128]{2,0,1:T(8,128)S(1)}, f32[256,4]{0,1:T(4,128)S(1)}, /*ind...) while((s32[]{:T(128)}, f32[256,4]{0,1:T(4,128)S(1)}, ...), condition=%wide.region_35.36_spmd, body=%wide.region_2.35_spmd.sunk | while | flops 2194940928 | bytes 91894560 | solution.py:145
  182.7 2.6 fusion.198
  185.4 1.9 conditional.24
  188.0 2.9 conditional.25
  190.9 2.9 conditional.26
  191.0 1.5 select_reduce_fusion.1
  193.9 1.9 conditional.27
  197.0 2.9 conditional.29
  200.1 2.9 conditional.31
  204.8 2.6 fusion.198
  207.4 1.9 conditional.24
  210.1 2.9 conditional.25
  213.0 2.9 conditional.26
  216.0 1.9 conditional.27
  219.1 2.9 conditional.29
  222.2 2.9 conditional.31
  226.9 2.6 fusion.198
  229.5 1.9 conditional.24
  232.1 2.9 conditional.25
  235.1 2.9 conditional.26
  235.1 1.5 select_reduce_fusion.1
  238.1 1.9 conditional.27
  241.2 2.9 conditional.29
  244.3 2.9 conditional.31
  249.0 2.6 fusion.198
  251.6 1.9 conditional.24
  254.2 2.9 conditional.25
  257.2 2.9 conditional.26
  260.2 1.9 conditional.27
  263.3 2.9 conditional.29
  266.3 2.9 conditional.31
  274.1 11.5 %convolution_convert_fusion = bf16[256,4096]{1,0:T(8,128)(2,1)} fusion(bf16[256,2048]{0,1:T(8,128)(2,1)S(1)} %bitcast_select_fusion, bf16[2048,4096]{1,0:T(8,128)(2,1)} %param.87), kind=kOutput, calls=%fused_computation.224 | convolution fusion | flops 4296015872 | bytes 19922944 | tf_op jit(solution)/shard_map/dot_general | solution.py:157
  285.7 31.2 %reduce-scatter.2.cloned.1.call-done = bf16[128,4096]{1,0:T(8,128)(2,1)} async-done(((bf16[256,4096]{1,0:T(8,128)(2,1)}), bf16[128,4096]{1,0:T(8,128)(2,1)}) %reduce-scatter.2.cloned.1.call-update) | async-done | bytes 1048592 | tf_op jit(solution)/shard_map/reduce_scatter | solution.py:156
  (516 shorter events, 97.3 us)
Async XLA Ops:
  6.5 11.7 %copy-start.20 = (s32[8]{0:T(128)S(1)}, s32[8]{0:T(128)}, u32[]{:S(2)}) copy-start(s32[8]{0:T(128)} %param.86) | copy-start | bytes 100
  6.5 11.8 %copy-start.21 = (s32[8]{0:T(128)S(1)}, s32[8]{0:T(128)}, u32[]{:S(2)}) copy-start(s32[8]{0:T(128)} %param.85) | copy-start | bytes 100
  6.5 11.9 %copy-start.16 = (bf16[256,2048]{1,0:T(8,128)(2,1)S(1)}, bf16[256,2048]{1,0:T(8,128)(2,1)}, u32[]{:S(2)}) copy-start(bf16[256,2048]{1,0:T(8,128)(2,1)} %param.81) | copy-start | bytes 3145732
  6.5 98.6 %all-reduce.2.cloned.1.call-start = ((), (), s32[]{:S(2)}) async-start(), calls=%async_computation.2 | async-start | bytes 524288 | tf_op jit(solution)/shard_map/psum | solution.py:17
  9.4 171.1 %all-gather.2.cloned.1.call-start = ((), (), s32[]{:S(2)}) async-start(), calls=%async_computation.1 | async-start | bytes 8912896 | tf_op jit(solution)/shard_map/all_gather | solution.py:106
  10.2 306.7 %reduce-scatter.2.cloned.1.call-start = ((), (), s32[]{:S(2)}) async-start(), calls=%async_computation.3 | async-start | bytes 3145728 | tf_op jit(solution)/shard_map/reduce_scatter | solution.py:156
  10.2 96.6 %collective-permute-start = (bf16[256,1024]{1,0:T(8,128)(2,1)}, bf16[256,1024]{1,0:T(8,128)(2,1)}, u32[]{:S(2)}, u32[]{:S(2)}) collective-permute-start(bf16[256,1024]{1,0:T(8,128)(2,1)} %copy-done.15), channel_id=1, source_target_pairs={{0,8},{2,10},{4,12},{6,14},{8,16},{10,18},{12,20},{14,22},{16,24},... | collective-permute-start | bytes 1572872 | tf_op jit(solution)/shard_map/ppermute | solution.py:23
  11.5 97.2 %collective-permute-start.1 = (bf16[256,1024]{1,0:T(8,128)(2,1)}, bf16[256,1024]{1,0:T(8,128)(2,1)}, u32[]{:S(2)}, u32[]{:S(2)}) collective-permute-start(bf16[256,1024]{1,0:T(8,128)(2,1)} %copy-done.15), channel_id=1, source_target_pairs={{0,6},{2,8},{4,10},{6,12},{8,14},{10,16},{12,18},{14,20},{16,22},{... | collective-permute-start | bytes 1572872 | tf_op jit(solution)/shard_map/ppermute | solution.py:23
  14.4 96.3 %collective-permute-start.2 = (bf16[256,1024]{1,0:T(8,128)(2,1)}, bf16[256,1024]{1,0:T(8,128)(2,1)}, u32[]{:S(2)}, u32[]{:S(2)}) collective-permute-start(bf16[256,1024]{1,0:T(8,128)(2,1)} %copy-done.15), channel_id=1, source_target_pairs={{0,4},{2,6},{4,8},{6,10},{8,12},{10,14},{12,16},{14,18},{16,20},{1... | collective-permute-start | bytes 1572872 | tf_op jit(solution)/shard_map/ppermute | solution.py:23
  16.3 96.3 %collective-permute-start.3 = (bf16[256,1024]{1,0:T(8,128)(2,1)}, bf16[256,1024]{1,0:T(8,128)(2,1)}, u32[]{:S(2)}, u32[]{:S(2)}) collective-permute-start(bf16[256,1024]{1,0:T(8,128)(2,1)} %copy-done.15), channel_id=1, source_target_pairs={{0,2},{2,4},{4,6},{6,8},{8,10},{10,12},{12,14},{14,16},{16,18},{18... | collective-permute-start | bytes 1572872 | tf_op jit(solution)/shard_map/ppermute | solution.py:23
  30.6 8.2 %copy-start.14 = (bf16[256,4,128]{0,2,1:T(8,128)(2,1)S(1)}, bf16[256,4,128]{0,2,1:T(8,128)(2,1)}, u32[]{:S(2)}) copy-start(bf16[256,4,128]{0,2,1:T(8,128)(2,1)} %get-tuple-element.1675) | copy-start | bytes 786436
  106.8 7.6 %copy-start.17 = (bf16[256,512]{1,0:T(8,128)(2,1)S(1)}, bf16[256,512]{1,0:T(8,128)(2,1)}, u32[]{:S(2)}) copy-start(bf16[256,512]{1,0:T(8,128)(2,1)} %param.82) | copy-start | bytes 786436
  108.8 6.4 %copy-start.18 = (bf16[256,512]{1,0:T(8,128)(2,1)S(1)}, bf16[256,512]{1,0:T(8,128)(2,1)}, u32[]{:S(2)}) copy-start(bf16[256,512]{1,0:T(8,128)(2,1)} %param.83) | copy-start | bytes 786436
  181.8 3.6 %copy-start.2 = (bf16[256,4,128]{2,0,1:T(8,128)(2,1)}, bf16[256,4,128]{2,0,1:T(8,128)(2,1)S(1)}, u32[]{:S(2)}) copy-start(bf16[256,4,128]{2,0,1:T(8,128)(2,1)S(1)} %get-tuple-element.2114) | copy-start | bytes 786436 | tf_op jit(solution)/shard_map/while
  185.4 1.3 copy-start.11
  188.0 2.2 copy-start.9
  190.9 3.0 copy-start.4
  190.9 2.2 copy-start.12
  193.9 1.3 copy-start.10
  197.0 2.2 copy-start.5
  200.1 3.8 %copy-start.3 = (bf16[256,4,128]{2,0,1:T(8,128)(2,1)S(1)}, bf16[256,4,128]{2,0,1:T(8,128)(2,1)}, u32[]{:S(2)}) copy-start(bf16[256,4,128]{2,0,1:T(8,128)(2,1)} %copy-done.2) | copy-start | bytes 786436 | tf_op jit(solution)/shard_map/while
  200.1 2.2 copy-start.6
  203.9 3.6 %copy-start.2 = (bf16[256,4,128]{2,0,1:T(8,128)(2,1)}, bf16[256,4,128]{2,0,1:T(8,128)(2,1)S(1)}, u32[]{:S(2)}) copy-start(bf16[256,4,128]{2,0,1:T(8,128)(2,1)S(1)} %get-tuple-element.2114) | copy-start | bytes 786436 | tf_op jit(solution)/shard_map/while
  210.1 2.2 copy-start.9
  213.0 3.0 copy-start.4
  213.0 2.2 copy-start.12
  216.0 1.3 copy-start.10
  219.1 2.2 copy-start.5
  222.2 3.8 %copy-start.3 = (bf16[256,4,128]{2,0,1:T(8,128)(2,1)S(1)}, bf16[256,4,128]{2,0,1:T(8,128)(2,1)}, u32[]{:S(2)}) copy-start(bf16[256,4,128]{2,0,1:T(8,128)(2,1)} %copy-done.2) | copy-start | bytes 786436 | tf_op jit(solution)/shard_map/while
  222.2 2.2 copy-start.6
  225.9 3.6 %copy-start.2 = (bf16[256,4,128]{2,0,1:T(8,128)(2,1)}, bf16[256,4,128]{2,0,1:T(8,128)(2,1)S(1)}, u32[]{:S(2)}) copy-start(bf16[256,4,128]{2,0,1:T(8,128)(2,1)S(1)} %get-tuple-element.2114) | copy-start | bytes 786436 | tf_op jit(solution)/shard_map/while
  229.5 1.3 copy-start.11
  232.2 2.2 copy-start.9
  235.1 3.0 copy-start.4
  235.1 2.2 copy-start.12
  238.1 1.3 copy-start.10
  241.2 2.2 copy-start.5
  244.2 3.8 %copy-start.3 = (bf16[256,4,128]{2,0,1:T(8,128)(2,1)S(1)}, bf16[256,4,128]{2,0,1:T(8,128)(2,1)}, u32[]{:S(2)}) copy-start(bf16[256,4,128]{2,0,1:T(8,128)(2,1)} %copy-done.2) | copy-start | bytes 786436 | tf_op jit(solution)/shard_map/while
  244.3 2.2 copy-start.6
  248.0 3.6 %copy-start.2 = (bf16[256,4,128]{2,0,1:T(8,128)(2,1)}, bf16[256,4,128]{2,0,1:T(8,128)(2,1)S(1)}, u32[]{:S(2)}) copy-start(bf16[256,4,128]{2,0,1:T(8,128)(2,1)S(1)} %get-tuple-element.2114) | copy-start | bytes 786436 | tf_op jit(solution)/shard_map/while
  251.6 1.3 copy-start.11
  254.2 2.2 copy-start.9
  257.2 3.0 copy-start.4
  257.2 2.2 copy-start.12
  260.2 1.3 copy-start.10
  263.3 2.2 copy-start.5
  266.3 3.8 %copy-start.3 = (bf16[256,4,128]{2,0,1:T(8,128)(2,1)S(1)}, bf16[256,4,128]{2,0,1:T(8,128)(2,1)}, u32[]{:S(2)}) copy-start(bf16[256,4,128]{2,0,1:T(8,128)(2,1)} %copy-done.2) | copy-start | bytes 786436 | tf_op jit(solution)/shard_map/while
  266.4 2.2 copy-start.6
  (12 other events, 11.9 us)
Sparse Core Ops, SparseCore 0:
  10.7 94.3 all-reduce.1
  107.3 73.1 all-gather.1
  285.8 30.9 reduce-scatter.1
where the time goes:
time: 327 us; the launch traced here: 324 us
  waiting for transfers between devices  150 us (46%)
  matrix products  60.8 us (19%)
  local copies, waits for them, and re-layouts  44.7 us (14%)
  other arithmetic  33.1 us (10%)
  between operations  18.8 us (6%)
  loops' own time  8.48 us (3%)
  starting transfers between devices  8.08 us (2%)
    psum x1, waiting for transfers between devices, spread(): return lax.psum(block, axis)  65.5 us
    all_gather x1, waiting for transfers between devices, body(): piece_rows = lax.all_gather(kv_pairs, 'ctx', axis=0, tiled=True)  52.4 us
    dot_general x25, matrix products, softmax_update(): jnp.einsum('rgd,kd->rgk', query_rows, key_rows, preferred_element_type=jn...  31.3 us
    reduce_scatter x1, waiting for transfers between devices, body(): lax.psum_scatter(jnp.dot(attention, w_out, preferred_element_type=jnp.flo...  31.2 us
    dot_general x25, matrix products, softmax_update(): jnp.einsum('rgk,kd->rgd', weights.astype(jnp.bfloat16), value_rows, prefe...  18.1 us
    reduce_sum x25, other arithmetic, softmax_update(): new_sum = running_sum * factor + jnp.sum(weights, axis=2)  17.4 us
    unnamed x26, local copies, waits for them, and re-layouts  12.5 us
    dot_general x1, matrix products, body(): jnp.dot(attention, w_out, preferred_element_type=jnp.float32)  11.5 us
  transfers between devices with their start and end apart: 7, of which 3 were waited for; matrix products, arithmetic and copies ran while one was open for 12% of the time, Pallas kernels for 0%

commit v1 on v0

v1 whole, which is shorter than its diff:
```python
import functools
import math

import jax
import jax.numpy as jnp
from jax import lax
from jax.experimental import pallas as pl
from jax.experimental.pallas import tpu as pltpu
from jax.sharding import PartitionSpec as P

HD = 128
LANES = 4
CHUNK = 512
LOW = -1e30
MESH = pl.DeviceIdType.MESH


def layer_kernel(
    ctx_count, tp_count, kind_ref, sink_ref, window_ref, q_ref, k_ref, v_ref, w_hbm, out_ref,
    kv_buf, w_buf, top_ref, acc_ref, bias_ref, attn_ref, part_ref, send_buf, recv_buf, own_ref,
    w_sem, block_send, block_recv, sum_send, sum_recv,
):
    rank = lax.axis_index("ctx")
    tp_rank = lax.axis_index("tp")
    rows, kv_cols = k_ref.shape
    local_kv = kv_cols // HD
    group = q_ref.shape[1] // kv_cols
    planes = ctx_count // LANES
    plane = lax.div(rank, LANES)
    lane = lax.rem(rank, LANES)
    odd = lax.rem(lane, 2)
    high = lax.div(lane, 2)
    sibling = rank + 1 - 2 * odd
    across = rank + 2 - 4 * high
    factor = math.log2(math.e) / math.sqrt(HD)
    out_cols = w_buf.shape[1]
    chunks = out_cols // CHUNK
    share = rows // tp_count

    w_copy = pltpu.make_async_copy(w_hbm, w_buf, w_sem)
    w_copy.start()

    barrier = pltpu.get_barrier_semaphore()

    def greet(where):
        pl.semaphore_signal(barrier, inc=1, device_id=where, device_id_type=MESH)

    greet({"ctx": sibling})
    greet({"ctx": across})
    for step in range(1, tp_count):
        greet({"tp": lax.rem(tp_rank + step, tp_count)})

    @pl.when(plane > 0)
    def _():
        greet({"ctx": rank - LANES})

    @pl.when(plane < planes - 1)
    def _():
        greet({"ctx": rank + LANES})

    own_rows = pl.ds(pl.multiple_of(rank * rows, rows), rows)
    kv_buf[own_rows, :kv_cols] = k_ref[...]
    kv_buf[own_rows, kv_cols:] = v_ref[...]
    top_ref[...] = jnp.full_like(top_ref, LOW)
    acc_ref[...] = jnp.zeros_like(acc_ref)

    beside_planes = jnp.minimum(plane, 1) + jnp.minimum(planes - 1 - plane, 1)
    pl.semaphore_wait(barrier, 1 + tp_count + beside_planes)

    def block_copy(block, way, target):
        where = pl.ds(pl.multiple_of(block * rows, rows), rows)
        return pltpu.make_async_remote_copy(
            src_ref=kv_buf.at[where],
            dst_ref=kv_buf.at[where],
            send_sem=block_send.at[block, way],
            recv_sem=block_recv.at[block],
            device_id={"ctx": target},
            device_id_type=MESH,
        )

    def send_on(block):
        @pl.when(plane < planes - 1)
        def _():
            block_copy(block, 0, rank + LANES).start()

        block_copy(block, 2, across).start()
        block_copy(block, 1, sibling).start()

    def fold(first_block):
        span = 2 * rows
        key_rows = pl.ds(pl.multiple_of(first_block * rows, rows), span)
        parts = span // HD

        def head_step(head, carry):
            index = tp_rank * local_kv + head
            reach = jnp.where(kind_ref[index] == 1, jnp.int32(2**30), window_ref[index])
            key_pos = first_block * rows + lax.broadcasted_iota(jnp.int32, (rows, span), 1)
            behind = key_pos - rank * rows - lax.broadcasted_iota(jnp.int32, (rows, span), 0)
            allowed = (behind <= 0) & ((behind > -reach) | (key_pos < sink_ref[index]))
            bias_ref[...] = jnp.where(allowed, 0.0, LOW)
            key_block = kv_buf[key_rows, pl.ds(pl.multiple_of(head * HD, HD), HD)]
            value_block = kv_buf[key_rows, pl.ds(pl.multiple_of(kv_cols + head * HD, HD), HD)]
            value_block = jnp.concatenate([value_block, jnp.ones_like(value_block)], axis=1)
            for member in range(group):
                slot = head * group + member
                query = q_ref[:, pl.ds(pl.multiple_of(slot * HD, HD), HD)]
                scores = lax.dot_general(
                    query, key_block, (((1,), (1,)), ((), ())),
                    preferred_element_type=jnp.float32,
                )
                scores = scores * factor + bias_ref[...]
                before = top_ref[slot]
                top = jnp.maximum(before, jnp.max(scores, axis=1, keepdims=True))
                weights = jnp.concatenate(
                    [
                        jnp.exp2(scores[:, i * HD : (i + 1) * HD] - top).astype(jnp.bfloat16)
                        for i in range(parts)
                    ],
                    axis=1,
                )
                keep = jnp.exp2(before - top)
                blended = jnp.dot(weights, value_block, preferred_element_type=jnp.float32)
                top_ref[slot] = top
                acc_ref[slot, :, :HD] = acc_ref[slot, :, :HD] * keep + blended[:, :HD]
                acc_ref[slot, :, HD:] = acc_ref[slot, :, HD:] * keep + blended[:, HD:]
            return carry

        lax.fori_loop(0, local_kv, head_step, 0)

    send_on(rank)

    def plane_step(back, carry):
        mine = rank - back * LANES
        beside = sibling - back * LANES
        far = across - back * LANES
        far_beside = far + 1 - 2 * odd
        near_pair = mine - odd
        far_pair = far - odd

        @pl.when(back < plane)
        def _():
            block_copy(mine - LANES, 0, rank).wait_recv()
            send_on(mine - LANES)

        block_copy(beside, 0, rank).wait_recv()
        fold(near_pair)
        block_copy(far, 0, rank).wait_recv()
        block_copy(far, 1, sibling).start()
        block_copy(far_beside, 0, rank).wait_recv()

        @pl.when(far_pair <= rank)
        def _():
            fold(far_pair)

        return carry

    lax.fori_loop(0, plane + 1, plane_step, 0)

    for slot in range(local_kv * group):
        attn_ref[:, slot * HD : (slot + 1) * HD] = (
            acc_ref[slot, :, :HD] / acc_ref[slot, :, HD:]
        ).astype(jnp.bfloat16)
    w_copy.wait()

    def sum_copy(target, source, chunk):
        where = pl.ds(pl.multiple_of(chunk * CHUNK, CHUNK), CHUNK)
        return pltpu.make_async_remote_copy(
            src_ref=send_buf.at[pl.ds(pl.multiple_of(target * share, share), share), where],
            dst_ref=recv_buf.at[pl.ds(pl.multiple_of(source * share, share), share), where],
            send_sem=sum_send.at[target, chunk],
            recv_sem=sum_recv.at[source, chunk],
            device_id={"tp": target},
            device_id_type=MESH,
        )

    def project(chunk, carry):
        where = pl.ds(pl.multiple_of(chunk * CHUNK, CHUNK), CHUNK)
        part_ref[...] = jnp.dot(attn_ref[...], w_buf[:, where], preferred_element_type=jnp.float32)
        send_buf[:, where] = part_ref[...].astype(jnp.bfloat16)
        for step in range(1, tp_count):
            sum_copy(lax.rem(tp_rank + step, tp_count), tp_rank, chunk).start()
        own_ref[:, where] = part_ref[pl.ds(pl.multiple_of(tp_rank * share, share), share), :]
        return carry

    lax.fori_loop(0, chunks, project, 0)

    def collect(chunk, carry):
        where = pl.ds(pl.multiple_of(chunk * CHUNK, CHUNK), CHUNK)
        total = own_ref[:, where]
        for step in range(1, tp_count):
            source = lax.rem(tp_rank + step, tp_count)
            sum_copy(source, source, chunk).wait_recv()
            rows_from = pl.ds(pl.multiple_of(source * share, share), share)
            total = total + recv_buf[rows_from, where].astype(jnp.float32)
        out_ref[:, where] = total.astype(jnp.bfloat16)
        return carry

    lax.fori_loop(0, chunks, collect, 0)

    def drain(back, carry):
        mine = rank - back * LANES
        far = across - back * LANES

        @pl.when(plane < planes - 1)
        def _():
            block_copy(mine, 0, rank + LANES).wait_send()

        block_copy(mine, 2, across).wait_send()
        block_copy(mine, 1, sibling).wait_send()
        block_copy(far, 1, sibling).wait_send()
        return carry

    lax.fori_loop(0, plane + 1, drain, 0)

    def drain_sums(chunk, carry):
        for step in range(1, tp_count):
            sum_copy(lax.rem(tp_rank + step, tp_count), tp_rank, chunk).wait_send()
        return carry

    lax.fori_loop(0, chunks, drain_sums, 0)


def body(ctx_count, tp_count, queries, keys, values, head_kind, sink_len, window_len, w_out):
    rows, q_cols = queries.shape
    kv_cols = keys.shape[1]
    heads = q_cols // HD
    in_cols, out_cols = w_out.shape
    share = rows // tp_count
    chunks = out_cols // CHUNK
    vmem = pl.BlockSpec(memory_space=pltpu.VMEM)
    smem = pl.BlockSpec(memory_space=pltpu.SMEM)
    return pl.pallas_call(
        functools.partial(layer_kernel, ctx_count, tp_count),
        out_shape=jax.ShapeDtypeStruct((share, out_cols), jnp.bfloat16),
        in_specs=[smem, smem, smem, vmem, vmem, vmem, pl.BlockSpec(memory_space=pl.ANY)],
        out_specs=vmem,
        scratch_shapes=[
            pltpu.VMEM((ctx_count * rows, 2 * kv_cols), jnp.bfloat16),
            pltpu.VMEM((in_cols, out_cols), jnp.bfloat16),
            pltpu.VMEM((heads, rows, HD), jnp.float32),
            pltpu.VMEM((heads, rows, 2 * HD), jnp.float32),
            pltpu.VMEM((rows, 2 * rows), jnp.float32),
            pltpu.VMEM((rows, q_cols), jnp.bfloat16),
            pltpu.VMEM((rows, CHUNK), jnp.float32),
            pltpu.VMEM((rows, out_cols), jnp.bfloat16),
            pltpu.VMEM((rows, out_cols), jnp.bfloat16),
            pltpu.VMEM((share, out_cols), jnp.float32),
            pltpu.SemaphoreType.DMA,
            pltpu.SemaphoreType.DMA((ctx_count, 3)),
            pltpu.SemaphoreType.DMA((ctx_count,)),
            pltpu.SemaphoreType.DMA((tp_count, chunks)),
            pltpu.SemaphoreType.DMA((tp_count, chunks)),
        ],
        compiler_params=pltpu.CompilerParams(
            collective_id=0, has_side_effects=True, vmem_limit_bytes=56 * 2**20
        ),
    )(head_kind, sink_len, window_len, queries, keys, values, w_out)


def solution(mesh):
    in_specs = (P("ctx", "tp"), P("ctx", "tp"), P("ctx", "tp"), P(), P(), P(), P("tp", None))
    out_specs = P(("ctx", "tp"), None)
    run = functools.partial(body, mesh.shape["ctx"], mesh.shape["tp"])
    return jax.shard_map(run, mesh=mesh, in_specs=in_specs, out_specs=out_specs, check_vma=False)
```

time: 327 us -> 87.7 us (0.27)
  waiting for transfers between devices: 150 us -> 0 us
  Pallas kernels: 0 us -> 85.2 us
  matrix products: 60.8 us -> 0 us
  local copies, waits for them, and re-layouts: 44.7 us -> 2.29 us
  other arithmetic: 33.1 us -> 0 us
  between operations: 18.8 us -> 0.01 us
  loops' own time: 8.48 us -> 0 us
  starting transfers between devices: 8.08 us -> 0 us
    pallas_call x0 -> x1, Pallas kernels: none -> 85.2 us  [body(): pl.pallas_call(functools.partial(layer_kernel, ctx_count, tp_count), out_...]
    psum x1 -> x0, waiting for transfers between devices: 65.5 us -> none  [spread(): return lax.psum(block, axis)]
    dot_general x51 -> x0, matrix products: 60.8 us -> none  [the longest x25 31.3 us: softmax_update(): jnp.einsum('rgd,kd->rgk', query_rows, key_rows, preferred_element_type=jn...]
    all_gather x1 -> x0, waiting for transfers between devices: 52.4 us -> none  [body(): piece_rows = lax.all_gather(kv_pairs, 'ctx', axis=0, tiled=True)]
    reduce_scatter x1 -> x0, waiting for transfers between devices: 31.2 us -> none  [body(): lax.psum_scatter(jnp.dot(attention, w_out, preferred_element_type=jnp.flo...]
    reduce_sum x25 -> x0, other arithmetic: 17.4 us -> none  [softmax_update(): new_sum = running_sum * factor + jnp.sum(weights, axis=2)]
    slice x107 -> x0, local copies, waits for them, and re-layouts: 13.3 us -> none  [the longest x4 10.5 us: key_step(): value_cols = key_block[:, value_index * HD:(value_index + 1) * HD]]
    while x48 -> x0, local copies, waits for them, and re-layouts: 11.8 us -> none
  transfers between devices with their start and end apart: 7 -> 0, of which waited for: 3 -> 0; matrix products, arithmetic and copies ran while one was open for 12% -> 0% of each run, Pallas kernels for 0% -> 0%
where the time goes in v1:
time: 87.7 us; the launch traced here: 87.5 us
  Pallas kernels  85.2 us (97%)
  local copies, waits for them, and re-layouts  2.29 us (3%)
    pallas_call x1, Pallas kernels, body(): pl.pallas_call(functools.partial(layer_kernel, ctx_count, tp_count), out_...  85.2 us
    unnamed x1, local copies, waits for them, and re-layouts  2.29 us

profile of v1, /device:TPU:24, one launch (start us, length us, event | category | flops | bytes accessed | tf_op | source)
XLA Modules:
  0.0 87.5 jit_solution(6924685332601817867)
XLA Ops:
  0.0 85.2 %shard_map.73 = bf16[128,4096]{1,0:T(8,128)(2,1)} custom-call(s32[8]{0:T(128)} %kind_ref.1, s32[8]{0:T(128)} %sink_ref.1, s32[8]{0:T(128)} %window_ref.1, bf16[256,2048]{1,0:T(8,128)(2,1)} %q_ref.1, bf16[256,512]{1,0:T(8,128)(2,1)} %k_ref.1, bf16[256,512]{1,0:T(8,128)(2,1)} %v_ref.1, bf16[2048,4096]{1,0:T(8,128)(2,1)} %w_hbm.1), custom_call_target="tpu_custom_call" | custom-call | tf_op jit(solution)/shard_map/pallas_call | solution.py:232
  85.2 2.3 %copy.9 = bf16[128,4096]{1,0:T(8,128)(2,1)} copy(bf16[128,4096]{1,0:T(8,128)(2,1)} %shard_map.73) | data formatting | bytes 2097152

commit v2 on v1

--- a/solution.py
+++ b/solution.py
@@ -37,9 +37,6 @@
     chunks = out_cols // CHUNK
     share = rows // tp_count
 
-    w_copy = pltpu.make_async_copy(w_hbm, w_buf, w_sem)
-    w_copy.start()
-
     barrier = pltpu.get_barrier_semaphore()
 
     def greet(where):
@@ -61,8 +58,6 @@
     own_rows = pl.ds(pl.multiple_of(rank * rows, rows), rows)
     kv_buf[own_rows, :kv_cols] = k_ref[...]
     kv_buf[own_rows, kv_cols:] = v_ref[...]
-    top_ref[...] = jnp.full_like(top_ref, LOW)
-    acc_ref[...] = jnp.zeros_like(acc_ref)
 
     beside_planes = jnp.minimum(plane, 1) + jnp.minimum(planes - 1 - plane, 1)
     pl.semaphore_wait(barrier, 1 + tp_count + beside_planes)
@@ -128,6 +123,10 @@
         lax.fori_loop(0, local_kv, head_step, 0)
 
     send_on(rank)
+    w_copy = pltpu.make_async_copy(w_hbm, w_buf, w_sem)
+    w_copy.start()
+    top_ref[...] = jnp.full_like(top_ref, LOW)
+    acc_ref[...] = jnp.zeros_like(acc_ref)
 
     def plane_step(back, carry):
         mine = rank - back * LANES

time: 87.7 us -> 87.7 us (level)
  no operation moved by 1% of the time
where the time goes in v2:
time: 87.7 us; the launch traced here: 87.5 us
  Pallas kernels  85.2 us (97%)
  local copies, waits for them, and re-layouts  2.29 us (3%)
    pallas_call x1, Pallas kernels, body(): pl.pallas_call(functools.partial(layer_kernel, ctx_count, tp_count), out_...  85.2 us
    unnamed x1, local copies, waits for them, and re-layouts  2.29 us

profile of v2, /device:TPU:24, one launch (start us, length us, event | category | flops | bytes accessed | tf_op | source)
XLA Modules:
  0.0 87.5 jit_solution(516978960565107998)
XLA Ops:
  0.0 85.2 %shard_map.73 = bf16[128,4096]{1,0:T(8,128)(2,1)} custom-call(s32[8]{0:T(128)} %kind_ref.1, s32[8]{0:T(128)} %sink_ref.1, s32[8]{0:T(128)} %window_ref.1, bf16[256,2048]{1,0:T(8,128)(2,1)} %q_ref.1, bf16[256,512]{1,0:T(8,128)(2,1)} %k_ref.1, bf16[256,512]{1,0:T(8,128)(2,1)} %v_ref.1, bf16[2048,4096]{1,0:T(8,128)(2,1)} %w_hbm.1), custom_call_target="tpu_custom_call" | custom-call | tf_op jit(solution)/shard_map/pallas_call | solution.py:231
  85.2 2.3 %copy.9 = bf16[128,4096]{1,0:T(8,128)(2,1)} copy(bf16[128,4096]{1,0:T(8,128)(2,1)} %shard_map.73) | data formatting | bytes 2097152
